TPU v7x, 32 devices: a whole 2x2x4 slice. The times are simulated.
32 devices in a mesh: dp: 8 (over z, y), mp: 4 (over x, core).
Axes of the slice: x: 2, y: 2, z: 4, core: 2. Of those that a mesh axis runs over, the one named last changes fastest.
Arguments:
- features_in: bfloat16 [16, 24576], P(None, 'dp'), may hold values from -6 to 6
- w_in: bfloat16 [16, 1024], P(None, 'mp'), may hold values from -1.5 to 1.5
- w_mid: bfloat16 [1024, 1024], P(None, 'mp'), may hold values from -0.1875 to 0.1875
- w_out: bfloat16 [1024], P('mp'), may hold values from -0.1875 to 0.1875
- targets: float32 [24576], P('dp'), may hold values from -6 to 6
- valid_steps: int32 [256], P('dp'), may hold values from 16 to 96, as said below
Outputs:
- predicted_change: float32 [24576], P('dp')
Inputs may be any that keep to these rules, and one draw needn't show every extreme that they name: `valid_steps`: the last building has all 96 valid steps.
All inputs are finite; a program needn't handle non-finite values.
Results may differ from a plain program's by a relative error of at most 0.00037.
Values may be sent and summed in bfloat16 or wider, within the bound.
A program may use at most 64 MiB of HBM per device.

v0:
```python
import jax
import jax.numpy as jnp
from jax import lax
from jax.sharding import PartitionSpec as P

STEPS = 96
ITERS = 3


damping = 0.002


def pull_back(columns, back):
    return lax.dot_general(
        columns, back, (((0,), (0,)), ((), ())), preferred_element_type=jnp.float32
    )


def shards(features_in, w_in, w_mid, w_out, targets, valid_steps):
    out_weight = w_out.astype(jnp.float32)
    valid_count = lax.psum(jnp.sum(valid_steps).astype(jnp.float32), "dp")
    whole_input = lax.all_gather(w_in, "mp", axis=1, tiled=True)
    hidden_one = jnp.tanh(
        jnp.dot(features_in.T, whole_input, preferred_element_type=jnp.float32)
    ).astype(jnp.bfloat16)
    hidden_two = jnp.tanh(jnp.dot(hidden_one, w_mid, preferred_element_type=jnp.float32))
    slope_out = (1.0 - hidden_two * hidden_two) * out_weight
    predicted = lax.psum(jnp.sum(hidden_two * out_weight, axis=-1), "mp")
    step_mask = (
        (jnp.arange(STEPS, dtype=jnp.int32)[None, :] < valid_steps[:, None])
        .astype(jnp.float32)
        .reshape(-1)
    )
    row_weight = step_mask / valid_count
    error_rows = row_weight * (predicted - targets)
    grad_back = (error_rows[:, None] * slope_out).astype(jnp.bfloat16)

    def tangent(dir_bf16):
        partial_rows = jnp.sum(
            jnp.dot(hidden_one, dir_bf16, preferred_element_type=jnp.float32) * slope_out, axis=-1
        )
        return lax.psum(partial_rows, "mp")

    gradient = lax.psum(pull_back(hidden_one, grad_back), "dp")

    def spread(vector):
        return vector.astype(jnp.bfloat16)

    def inner_product(first, second):
        return lax.psum(jnp.sum(first * second), "mp")

    solution = jnp.zeros_like(gradient)
    remainder = -gradient
    direction = remainder
    norm_now = inner_product(remainder, remainder)
    for iteration in range(ITERS):
        summed = lax.psum(
            pull_back(
                hidden_one,
                ((row_weight * tangent(spread(direction)))[:, None] * slope_out).astype(
                    jnp.bfloat16
                ),
            ),
            "dp",
        )
        curved = summed + damping * direction
        step_size = norm_now / inner_product(direction, curved)
        solution = solution + step_size * direction
        remainder = remainder - step_size * curved
        if iteration + 1 < ITERS:
            norm_next = inner_product(remainder, remainder)
            direction = remainder + norm_next / norm_now * direction
            norm_now = norm_next
    return tangent(spread(solution))


def solution(mesh):
    return jax.shard_map(
        shards,
        mesh=mesh,
        in_specs=(P(None, "dp"), P(None, "mp"), P(None, "mp"), P("mp"), P("dp"), P("dp")),
        out_specs=P("dp"),
        check_vma=False,
    )
```

profile of v0, /device:TPU:0, one launch (start us, length us, event | category | flops | bytes accessed | tf_op | source)
XLA Modules:
  0.0 518.2 jit_solution(10270129785186823184)
XLA Ops:
  8.5 23.6 %psum.112 = f32[]{:T(128)} all-reduce(f32[]{:T(128)S(6)} %convert_element_type.36), channel_id=1, replica_groups=mesh['dp'=8,'mp'=4] {'dp'}, use_global_device_ids=true, to_apply=%region_1.0 | all-reduce | flops 1 | bytes 8 | tf_op jit(solution)/shard_map/psum | solution.py:21
  34.3 5.4 %all_gather.3 = bf16[16,1024]{1,0:T(8,128)(2,1)S(1)} all-gather(bf16[16,256]{1,0:T(8,128)(2,1)} %param.7), channel_id=1, replica_groups=mesh['dp'=8,'mp'=4] {'mp'}, dimensions={1}, use_global_device_ids=true | all-gather | bytes 40960 | tf_op jit(solution)/shard_map/all_gather | solution.py:22
  39.7 2.7 tanh_convert_fusion
  42.5 3.8 multiply_reduce_fusion
  46.3 11.3 %psum.113 = f32[3072]{0:T(1024)S(1)} all-reduce(f32[3072]{0:T(1024)S(1)} %get-tuple-element.11), channel_id=1, replica_groups=mesh['dp'=8,'mp'=4] {'mp'}, use_global_device_ids=true, to_apply=%region_3.0 | all-reduce | flops 3072 | bytes 24576 | tf_op jit(solution)/shard_map/psum | solution.py:28
  57.6 6.7 %fusion = f32[1024,256]{1,0:T(8,128)} fusion(bf16[3072,1024]{1,0:T(8,128)(2,1)} %copy-done.1, f32[3072]{0:T(1024)S(1)} %subtract_multiply_fusion.1, f32[3072,256]{0,1:T(8,128)} %get-tuple-element.12, f32[256]{0:T(256)S(1)} %convert_element_type.37), kind=kOutput, calls=%fused_computation.12 | convolution fusion | flops 1614544896 | bytes 10499072 | tf_op jit(solution)/shard_map/dot_general | solution.py:14
  64.4 74.4 %all-reduce.6.cloned.1.call-done = f32[1024,256]{1,0:T(8,128)} async-done(((f32[1024,256]{1,0:T(8,128)}), f32[1024,256]{1,0:T(8,128)}) %all-reduce.6.cloned.1.call-update) | async-done | bytes 1048592 | tf_op jit(solution)/shard_map/psum | solution.py:44
  138.8 6.2 %fusion.8 = f32[3072]{0:T(1024)S(1)} fusion(bf16[3072,1024]{1,0:T(8,128)(2,1)} %copy-done.1, f32[1024,256]{1,0:T(8,128)} %all-reduce.6.cloned.1.call-done, f32[256]{0:T(256)S(1)} %convert_element_type.37, f32[3072,256]{0,1:T(8,128)} %get-tuple-element.12), kind=kOutput, calls=%fused_computation.20 | convolution fusion | flops 1615066112 | bytes 10499072 | tf_op jit(solution)/shard_map/dot_general | solution.py:40
  145.0 10.2 %psum.116 = f32[3072]{0:T(1024)S(1)} all-reduce(f32[3072]{0:T(1024)S(1)} %fusion.8), channel_id=1, replica_groups=mesh['dp'=8,'mp'=4] {'mp'}, use_global_device_ids=true, to_apply=%region_8.0 | all-reduce | flops 3072 | bytes 24576 | tf_op jit(solution)/shard_map/psum | solution.py:42
  155.2 6.8 %fusion.1 = f32[1024,256]{1,0:T(8,128)} fusion(bf16[3072,1024]{1,0:T(8,128)(2,1)} %copy-done.1, f32[3072]{0:T(1024)S(1)} %mul.147, f32[3072,256]{0,1:T(8,128)} %get-tuple-element.12, f32[256]{0:T(256)S(1)} %convert_element_type.37), kind=kOutput, calls=%fused_computation.13 | convolution fusion | flops 1614544896 | bytes 10499072 | tf_op jit(solution)/shard_map/dot_general | solution.py:14
  162.2 77.6 %all-reduce.8.cloned.1.call-done = f32[1024,256]{1,0:T(8,128)} async-done(((f32[1024,256]{1,0:T(8,128)}), f32[1024,256]{1,0:T(8,128)}) %all-reduce.8.cloned.1.call-update) | async-done | bytes 1048592 | tf_op jit(solution)/shard_map/psum | solution.py:57
  239.9 2.2 multiply_reduce_fusion.5
  242.0 6.5 %all-reduce = (f32[]{:T(128)}, f32[]{:T(128)}) all-reduce(f32[]{:T(128)} %get-tuple-element.6, f32[]{:T(128)} %get-tuple-element.5), channel_id=1, replica_groups=mesh['dp'=8,'mp'=4] {'mp'}, use_global_device_ids=true, to_apply=%region_6.0 | all-reduce | flops 2 | bytes 16 | tf_op jit(solution)/shard_map/psum | solution.py:50
  249.8 2.1 multiply_reduce_fusion.4
  251.9 7.0 %psum.119 = f32[]{:T(128)} all-reduce(f32[]{:T(128)} %get-tuple-element.9), channel_id=1, replica_groups=mesh['dp'=8,'mp'=4] {'mp'}, use_global_device_ids=true, to_apply=%region_13.0 | all-reduce | flops 1 | bytes 8 | tf_op jit(solution)/shard_map/psum | solution.py:50
  262.4 5.1 fusion.9
  267.6 10.2 %psum.120 = f32[3072]{0:T(1024)S(1)} all-reduce(f32[3072]{0:T(1024)S(1)} %fusion.9), channel_id=1, replica_groups=mesh['dp'=8,'mp'=4] {'mp'}, use_global_device_ids=true, to_apply=%region_15.0 | all-reduce | flops 3072 | bytes 24576 | tf_op jit(solution)/shard_map/psum | solution.py:42
  277.8 6.7 %fusion.2 = f32[1024,256]{1,0:T(8,128)} fusion(bf16[3072,1024]{1,0:T(8,128)(2,1)} %copy-done.1, f32[3072]{0:T(1024)S(1)} %mul.159, f32[3072,256]{0,1:T(8,128)} %get-tuple-element.12, f32[256]{0:T(256)S(1)} %convert_element_type.37), kind=kOutput, calls=%fused_computation.14 | convolution fusion | flops 1614544896 | bytes 10499072 | tf_op jit(solution)/shard_map/dot_general | solution.py:14
  284.6 77.0 %all-reduce.10.cloned.1.call-done = f32[1024,256]{1,0:T(8,128)} async-done(((f32[1024,256]{1,0:T(8,128)}), f32[1024,256]{1,0:T(8,128)}) %all-reduce.10.cloned.1.call-update) | async-done | bytes 1048592 | tf_op jit(solution)/shard_map/psum | solution.py:57
  361.6 2.1 multiply_reduce_fusion.3
  363.7 6.5 %psum.122 = f32[]{:T(128)} all-reduce(f32[]{:T(128)} %multiply_reduce_fusion.3), channel_id=1, replica_groups=mesh['dp'=8,'mp'=4] {'mp'}, use_global_device_ids=true, to_apply=%region_18.0 | all-reduce | flops 1 | bytes 8 | tf_op jit(solution)/shard_map/psum | solution.py:50
  371.5 2.1 multiply_reduce_fusion.2
  373.6 7.0 %psum.123 = f32[]{:T(128)} all-reduce(f32[]{:T(128)} %multiply_reduce_fusion.2), channel_id=1, replica_groups=mesh['dp'=8,'mp'=4] {'mp'}, use_global_device_ids=true, to_apply=%region_20.0 | all-reduce | flops 1 | bytes 8 | tf_op jit(solution)/shard_map/psum | solution.py:50
  381.9 1.6 multiply_add_fusion
  384.5 5.2 fusion.10
  389.6 10.2 %psum.124 = f32[3072]{0:T(1024)S(1)} all-reduce(f32[3072]{0:T(1024)S(1)} %fusion.10), channel_id=1, replica_groups=mesh['dp'=8,'mp'=4] {'mp'}, use_global_device_ids=true, to_apply=%region_22.0 | all-reduce | flops 3072 | bytes 24576 | tf_op jit(solution)/shard_map/psum | solution.py:42
  399.8 6.8 %fusion.3 = f32[1024,256]{1,0:T(8,128)} fusion(bf16[3072,1024]{1,0:T(8,128)(2,1)} %copy-done.1, f32[3072]{0:T(1024)S(1)} %mul.171, f32[3072,256]{0,1:T(8,128)} %get-tuple-element.12, f32[256]{0:T(256)S(1)} %convert_element_type.37), kind=kOutput, calls=%fused_computation.15 | convolution fusion | flops 1614544896 | bytes 10499072 | tf_op jit(solution)/shard_map/dot_general | solution.py:14
  406.7 77.1 %all-reduce.12.cloned.1.call-done = f32[1024,256]{1,0:T(8,128)} async-done(((f32[1024,256]{1,0:T(8,128)}), f32[1024,256]{1,0:T(8,128)}) %all-reduce.12.cloned.1.call-update) | async-done | bytes 1048592 | tf_op jit(solution)/shard_map/psum | solution.py:57
  483.7 2.4 multiply_reduce_fusion.1
  486.2 6.7 %psum.126 = f32[]{:T(128)} all-reduce(f32[]{:T(128)} %multiply_reduce_fusion.1), channel_id=1, replica_groups=mesh['dp'=8,'mp'=4] {'mp'}, use_global_device_ids=true, to_apply=%region_25.0 | all-reduce | flops 1 | bytes 8 | tf_op jit(solution)/shard_map/psum | solution.py:50
  494.1 6.3 %fusion.11 = f32[3072]{0:T(1024)S(1)} fusion(bf16[3072,1024]{1,0:T(8,128)(2,1)} %copy-done.1, f32[1024,256]{1,0:T(8,128)} %copy-done.4, f32[1024,256]{1,0:T(8,128)S(1)} %multiply_add_fusion.2, f32[1024,256]{1,0:T(8,128)S(1)} %copy-done.3, f32[]{:T(128)S(6)} %div.30, f32[]{:T(128)S(6)} %div.28, f32[]{:T(128)S(6)} %div.26, f32[256]{0:T(256)S(1)} %convert_element_type.37, ...), kind=kOutput, calls=%fused_computation.23 | convolution fusion | flops 1616376832 | bytes 12596236 | tf_op jit(solution)/shard_map/dot_general | solution.py:40
  500.4 11.2 %psum.127 = f32[3072]{0:T(1024)} all-reduce(f32[3072]{0:T(1024)S(1)} %fusion.11), channel_id=1, replica_groups=mesh['dp'=8,'mp'=4] {'mp'}, use_global_device_ids=true, to_apply=%region_27.0 | all-reduce | flops 3072 | bytes 24576 | tf_op jit(solution)/shard_map/psum | solution.py:42
  (33 shorter events, 6.4 us)
Async XLA Ops:
  6.5 35.9 %copy-start = (bf16[1024,256]{1,0:T(8,128)(2,1)S(1)}, bf16[1024,256]{1,0:T(8,128)(2,1)}, u32[]{:S(2)}) copy-start(bf16[1024,256]{1,0:T(8,128)(2,1)} %param.8) | copy-start | bytes 1572868
  6.5 132.2 %all-reduce.6.cloned.1.call-start = ((), (), s32[]{:S(2)}) async-start(), calls=%async_computation | async-start | bytes 2097152 | tf_op jit(solution)/shard_map/psum | solution.py:44
  42.5 3.8 copy-start.1
  42.5 15.1 %copy-start.5 = (f32[3072]{0:T(1024)S(1)}, f32[3072]{0:T(1024)}, u32[]{:S(2)}) copy-start(f32[3072]{0:T(1024)} %param.10) | copy-start | bytes 36868
  64.3 175.5 %all-reduce.8.cloned.1.call-start = ((), (), s32[]{:S(2)}) async-start(), calls=%async_computation.1 | async-start | bytes 2097152 | tf_op jit(solution)/shard_map/psum | solution.py:57
  155.2 84.7 %copy-start.2 = (f32[1024,256]{1,0:T(8,128)S(1)}, f32[1024,256]{1,0:T(8,128)}, u32[]{:S(2)}) copy-start(f32[1024,256]{1,0:T(8,128)} %all-reduce.6.cloned.1.call-done) | copy-start | bytes 3145732
  162.0 199.6 %all-reduce.10.cloned.1.call-start = ((), (), s32[]{:S(2)}) async-start(), calls=%async_computation.2 | async-start | bytes 2097152 | tf_op jit(solution)/shard_map/psum | solution.py:57
  260.2 2.2 copy-start.6
  284.5 199.2 %all-reduce.12.cloned.1.call-start = ((), (), s32[]{:S(2)}) async-start(), calls=%async_computation.3 | async-start | bytes 2097152 | tf_op jit(solution)/shard_map/psum | solution.py:57
  381.9 2.6 copy-start.7
  383.5 1.0 copy-start.4
  406.6 87.5 %copy-start.3 = (f32[1024,256]{1,0:T(8,128)S(1)}, f32[1024,256]{1,0:T(8,128)}, u32[]{:S(2)}) copy-start(f32[1024,256]{1,0:T(8,128)} %all-reduce.6.cloned.1.call-done) | copy-start | bytes 3145732
Sparse Core Ops, SparseCore 0:
  64.5 74.2 all-reduce.5
  162.1 77.7 all-reduce.7
  284.6 76.9 all-reduce.9
  406.8 76.9 all-reduce.11
where the time goes:
time: 519 us; the launch traced here: 518 us
  waiting for transfers between devices  306 us (59%)
  blocking collectives  116 us (22%)
  matrix products  56.2 us (11%)
  between operations  21 us (4%)
  other arithmetic  16.8 us (3%)
    psum x3, waiting for transfers between devices, shards(): lax.psum(pull_back(hidden_one, ((row_weight * tangent(spread(direction)))...  232 us
    psum x1, waiting for transfers between devices, shards(): gradient = lax.psum(pull_back(hidden_one, grad_back), 'dp')  74.4 us
    psum x4, blocking collectives, tangent(): return lax.psum(partial_rows, 'mp')  41.8 us
    psum x5, blocking collectives, inner_product(): return lax.psum(jnp.sum(first * second), 'mp')  33.7 us
    dot_general x4, matrix products, pull_back(): lax.dot_general(columns, back, (((0,), (0,)), ((), ())), preferred_elemen...  27 us
    psum x1, blocking collectives, shards(): valid_count = lax.psum(jnp.sum(valid_steps).astype(jnp.float32), 'dp')  23.6 us
    dot_general x4, matrix products, tangent(): jnp.dot(hidden_one, dir_bf16, preferred_element_type=jnp.float32)  22.8 us
    psum x1, blocking collectives, shards(): predicted = lax.psum(jnp.sum(hidden_two * out_weight, axis=-1), 'mp')  11.3 us
  transfers between devices with their start and end apart: 4, of which 4 were waited for; matrix products, arithmetic and copies ran while one was open for 0% of the time, Pallas kernels for 0%

commit v1 on v0

v1 whole, which is shorter than its diff:
```python
import functools

import jax
import jax.numpy as jnp
from jax import lax
from jax.experimental import pallas as pl
from jax.experimental.pallas import tpu as pltpu
from jax.sharding import PartitionSpec as P

STEPS = 96
damping = 0.002
MESH = pl.DeviceIdType.MESH
NT = (((1,), (1,)), ((), ()))
TN = (((0,), (0,)), ((), ()))


def tile_of(rows):
    return 512 if rows % 512 == 0 else 128


def kernel(
    nd, nm, feat, win, wmid, wout, targ, vs, out,
    win_all, h1t, st, ust, u_row, wmid_t, v_t, rows_out, rows_in, scal_out, scal_in,
    p_out, p_in, v_all, own, r_p, d_p, q_p,
    win_ss, win_rs, row_ss, row_rs, scal_ss, scal_rs, p_ss, p_rs, v_ss, v_rs,
):
    hidden, cols = wmid.shape
    rows = feat.shape[1]
    piece = hidden // nd
    tile = tile_of(rows)
    tiles = rows // tile
    dp = lax.axis_index("dp")
    mp = lax.axis_index("mp")

    barrier = pltpu.get_barrier_semaphore()

    @pl.loop(1, nd)
    def _(d):
        pl.semaphore_signal(
            barrier, inc=1, device_id=(lax.rem(dp + d, nd), mp), device_id_type=MESH
        )

    @pl.loop(1, nm)
    def _(d):
        pl.semaphore_signal(
            barrier, inc=1, device_id=(dp, lax.rem(mp + d, nm)), device_id_type=MESH
        )

    pl.semaphore_wait(barrier, nd - 1 + nm - 1)

    def win_copy(d):
        return pltpu.make_async_remote_copy(
            src_ref=win, dst_ref=win_all.at[d], send_sem=win_ss.at[d], recv_sem=win_rs.at[d],
            device_id=(dp, lax.rem(mp + d, nm)), device_id_type=MESH,
        )

    def row_copy(rnd, d):
        return pltpu.make_async_remote_copy(
            src_ref=rows_out.at[rnd], dst_ref=rows_in.at[rnd, d],
            send_sem=row_ss.at[rnd, d], recv_sem=row_rs.at[rnd, d],
            device_id=(dp, lax.rem(mp + d, nm)), device_id_type=MESH,
        )

    def scal_copy(rnd, d):
        return pltpu.make_async_remote_copy(
            src_ref=scal_out.at[rnd], dst_ref=scal_in.at[rnd, d],
            send_sem=scal_ss.at[rnd, d], recv_sem=scal_rs.at[rnd, d],
            device_id=(lax.rem(dp + d, nd), mp), device_id_type=MESH,
        )

    def p_copy(rnd, d):
        return pltpu.make_async_remote_copy(
            src_ref=p_out.at[rnd, d], dst_ref=p_in.at[rnd, d],
            send_sem=p_ss.at[rnd, d], recv_sem=p_rs.at[rnd, d],
            device_id=(lax.rem(dp + d, nd), mp), device_id_type=MESH,
        )

    def v_copy(rnd, d):
        mine = v_all.at[rnd, pl.ds(pl.multiple_of(dp * piece, piece), piece)]
        return pltpu.make_async_remote_copy(
            src_ref=mine, dst_ref=mine,
            send_sem=v_ss.at[rnd, d], recv_sem=v_rs.at[rnd, d],
            device_id=(lax.rem(dp + d, nd), mp), device_id_type=MESH,
        )

    def start(copy, n):
        @pl.loop(1, n)
        def _(d):
            copy(d).start()

    def finish(copy, n):
        @pl.loop(1, n)
        def _(d):
            copy(d).wait()

    def send_scalars(rnd, values):
        scal_out[rnd] = jnp.concatenate(
            [jnp.broadcast_to(v, (1, 128)) for v in values]
            + [jnp.zeros((8 - len(values), 128), jnp.float32)],
            axis=0,
        )
        start(functools.partial(scal_copy, rnd), nd)

    def sum_scalars(rnd):
        finish(functools.partial(scal_copy, rnd), nd)
        total = scal_out[rnd]
        for d in range(1, nd):
            total = total + scal_in[rnd, d]
        return total

    def sum_rows(rnd):
        start(functools.partial(row_copy, rnd), nm)
        finish(functools.partial(row_copy, rnd), nm)
        total = rows_out[rnd]
        for d in range(1, nm):
            total = total + rows_in[rnd, d]
        return total

    start(win_copy, nm)
    steps = vs[...]
    send_scalars(0, [jnp.sum(steps.astype(jnp.float32), axis=0, keepdims=True)])
    builds = vs.shape[0]
    offset = lax.broadcasted_iota(jnp.int32, (builds, rows), 1) - STEPS * (
        lax.broadcasted_iota(jnp.int32, (builds, rows), 0)
    )
    mask = jnp.sum(
        jnp.where((offset >= 0) & (offset < steps), 1.0, 0.0), axis=0, keepdims=True
    )
    wmid_t[...] = wmid[...].T
    win_all[0] = win[...]
    finish(win_copy, nm)

    @pl.loop(0, tiles)
    def _(i):
        at = pl.ds(pl.multiple_of(i * tile, tile), tile)
        block = feat[:, at]
        for d in range(nm):
            owner = lax.rem(mp + nm - d, nm)
            first = lax.dot_general(win_all[d], block, TN, preferred_element_type=jnp.float32)
            h1t[pl.ds(pl.multiple_of(owner * cols, cols), cols), at] = jnp.tanh(first).astype(
                jnp.bfloat16
            )
        two = jnp.tanh(jnp.dot(wmid_t[...], h1t[:, at], preferred_element_type=jnp.float32))
        weight = wout[...]
        st[:, at] = (1.0 - two * two) * weight
        rows_out[0, :, at] = jnp.sum(two * weight, axis=0, keepdims=True)

    def tangent(rnd):
        finish(functools.partial(v_copy, rnd), nd)
        v_t[...] = v_all[rnd].T

        @pl.loop(0, tiles)
        def _(i):
            at = pl.ds(pl.multiple_of(i * tile, tile), tile)
            z = jnp.dot(v_t[...], h1t[:, at], preferred_element_type=jnp.float32)
            rows_out[rnd + 1, :, at] = jnp.sum(z * st[:, at], axis=0, keepdims=True)

        return sum_rows(rnd + 1)

    def pull_back(rnd, row):
        u_row[...] = row

        @pl.loop(0, tiles)
        def _(i):
            at = pl.ds(pl.multiple_of(i * tile, tile), tile)
            ust[:, at] = (u_row[:, at] * st[:, at]).astype(jnp.bfloat16)

        def part(d):
            owner = lax.rem(dp + d, nd)
            left = h1t[pl.ds(pl.multiple_of(owner * piece, piece), piece), :]
            return lax.dot_general(left, ust[...], NT, preferred_element_type=jnp.float32)

        @pl.loop(1, nd)
        def _(d):
            p_out[rnd, d] = part(d).astype(jnp.bfloat16)
            p_copy(rnd, d).start()

        own[...] = part(0)
        finish(functools.partial(p_copy, rnd), nd)
        total = own[...]
        for d in range(1, nd):
            total = total + p_in[rnd, d].astype(jnp.float32)
        return total

    def spread(rnd):
        v_all[rnd, pl.ds(pl.multiple_of(dp * piece, piece), piece)] = r_p[...].astype(jnp.bfloat16)
        start(functools.partial(v_copy, rnd), nd)

    def dot(a, b):
        return jnp.sum(a * b, axis=1, keepdims=True)

    predicted = sum_rows(0)
    valid_count = sum_scalars(0)[0:1, 0:1]
    weight = mask / valid_count
    y_r = weight * (targ[...] - predicted)
    r_p[...] = pull_back(0, y_r)
    spread(0)
    t_r = tangent(0)
    wt = weight * t_r
    send_scalars(1, [dot(y_r, t_r), dot(wt, t_r)])
    q_p[...] = pull_back(1, wt)
    sums = sum_scalars(1)
    norm, curve = sums[0:1, 0:1], sums[1:2, 0:1]
    length = norm
    step = norm / (curve + damping * length)
    d_p[...] = r_p[...]
    r_p[...] = r_p[...] - step * (q_p[...] + damping * d_p[...])
    spread(1)
    t_d, y_d = t_r, y_r
    change = step * t_d
    y_r = y_r - step * (wt + damping * y_d)

    t_r = tangent(1)
    wt = weight * t_r
    send_scalars(2, [dot(y_r, t_r), dot(wt, t_r), dot(wt, t_d), dot(y_r, t_d)])
    back = pull_back(2, wt)
    sums = sum_scalars(2)
    beta = sums[0:1, 0:1] / norm
    norm = sums[0:1, 0:1]
    curve = sums[1:2, 0:1] + beta * (2.0 * sums[2:3, 0:1] + beta * curve)
    length = norm + beta * (2.0 * sums[3:4, 0:1] + beta * length)
    step = norm / (curve + damping * length)
    r_p[...] = r_p[...] - step * (
        back + beta * q_p[...] + damping * (r_p[...] + beta * d_p[...])
    )
    spread(2)
    t_d = t_r + beta * t_d
    y_d = y_r + beta * y_d
    change = change + step * t_d
    y_r = y_r - step * (weight * t_d + damping * y_d)

    t_r = tangent(2)
    wt = weight * t_r
    send_scalars(3, [dot(y_r, t_r), dot(wt, t_r), dot(wt, t_d), dot(y_r, t_d)])
    sums = sum_scalars(3)
    beta = sums[0:1, 0:1] / norm
    norm = sums[0:1, 0:1]
    curve = sums[1:2, 0:1] + beta * (2.0 * sums[2:3, 0:1] + beta * curve)
    length = norm + beta * (2.0 * sums[3:4, 0:1] + beta * length)
    step = norm / (curve + damping * length)
    t_d = t_r + beta * t_d
    out[...] = change + step * t_d


def shards(nd, nm, features_in, w_in, w_mid, w_out, targets, valid_steps):
    hidden, cols = w_mid.shape
    rows = features_in.shape[1]
    piece = hidden // nd
    vmem = pl.BlockSpec(memory_space=pltpu.VMEM)
    dma = pltpu.SemaphoreType.DMA
    bf16, f32 = jnp.bfloat16, jnp.float32
    change = pl.pallas_call(
        functools.partial(kernel, nd, nm),
        out_shape=jax.ShapeDtypeStruct((1, rows), f32),
        in_specs=[vmem] * 6,
        out_specs=vmem,
        scratch_shapes=[
            pltpu.VMEM((nm,) + w_in.shape, bf16),
            pltpu.VMEM((hidden, rows), bf16),
            pltpu.VMEM((cols, rows), f32),
            pltpu.VMEM((cols, rows), bf16),
            pltpu.VMEM((1, rows), f32),
            pltpu.VMEM((cols, hidden), bf16),
            pltpu.VMEM((cols, hidden), bf16),
            pltpu.VMEM((4, 1, rows), f32),
            pltpu.VMEM((4, nm, 1, rows), f32),
            pltpu.VMEM((4, 8, 128), f32),
            pltpu.VMEM((4, nd, 8, 128), f32),
            pltpu.VMEM((3, nd, piece, cols), bf16),
            pltpu.VMEM((3, nd, piece, cols), bf16),
            pltpu.VMEM((3, hidden, cols), bf16),
            pltpu.VMEM((piece, cols), f32),
            pltpu.VMEM((piece, cols), f32),
            pltpu.VMEM((piece, cols), f32),
            pltpu.VMEM((piece, cols), f32),
            dma((nm,)), dma((nm,)),
            dma((4, nm)), dma((4, nm)),
            dma((4, nd)), dma((4, nd)),
            dma((3, nd)), dma((3, nd)),
            dma((3, nd)), dma((3, nd)),
        ],
        compiler_params=pltpu.CompilerParams(
            collective_id=0, has_side_effects=True, vmem_limit_bytes=56 * 1024 * 1024
        ),
    )(
        features_in,
        w_in,
        w_mid,
        w_out.astype(f32).reshape(cols, 1),
        targets.reshape(1, rows),
        valid_steps.reshape(-1, 1),
    )
    return change.reshape(rows)


def solution(mesh):
    return jax.shard_map(
        functools.partial(shards, mesh.shape["dp"], mesh.shape["mp"]),
        mesh=mesh,
        in_specs=(P(None, "dp"), P(None, "mp"), P(None, "mp"), P("mp"), P("dp"), P("dp")),
        out_specs=P("dp"),
        check_vma=False,
    )
```

time: 519 us -> 129 us (0.25)
  waiting for transfers between devices: 306 us -> 0 us
  Pallas kernels: 0 us -> 125 us
  blocking collectives: 116 us -> 0 us
  matrix products: 56.2 us -> 0 us
  between operations: 21 us -> 0.01 us
  other arithmetic: 16.8 us -> 0.01 us
    psum x4 -> x0, waiting for transfers between devices: 306 us -> none  [the longest x3 232 us: shards(): lax.psum(pull_back(hidden_one, ((row_weight * tangent(spread(direction)))...]
    pallas_call x0 -> x1, Pallas kernels: none -> 125 us  [shards(): pl.pallas_call(functools.partial(kernel, nd, nm), out_shape=jax.ShapeDtyp...]
    psum x11 -> x0, blocking collectives: 110 us -> none  [the longest x4 41.8 us: tangent(): return lax.psum(partial_rows, 'mp')]
    dot_general x10 -> x0, matrix products: 56.2 us -> none  [the longest x4 27 us: pull_back(): lax.dot_general(columns, back, (((0,), (0,)), ((), ())), preferred_elemen...]
    reduce_sum x6 -> x0, other arithmetic: 12.3 us -> none  [the longest x5 10.9 us: inner_product(): return lax.psum(jnp.sum(first * second), 'mp')]
    all_gather x1 -> x0, blocking collectives: 5.4 us -> none  [shards(): whole_input = lax.all_gather(w_in, 'mp', axis=1, tiled=True)]
  transfers between devices with their start and end apart: 4 -> 0, of which waited for: 4 -> 0; matrix products, arithmetic and copies ran while one was open for 0% -> 0% of each run, Pallas kernels for 0% -> 0%
where the time goes in v1:
time: 129 us
  Pallas kernels  125 us (97%)
  local copies, waits for them, and re-layouts  4.08 us (3%)
    pallas_call x1, Pallas kernels, shards(): pl.pallas_call(functools.partial(kernel, nd, nm), out_shape=jax.ShapeDtyp...  125 us
    unnamed x5, local copies, waits for them, and re-layouts  2.62 us

profile of v1, /device:TPU:0, one launch (start us, length us, event | category | flops | bytes accessed | tf_op | source)
XLA Modules:
  0.0 128.8 jit_solution(580487406234932384)
XLA Ops:
  0.0 0.0 copy-start.1
  0.0 0.7 copy-done.1
  0.7 0.0 copy-start
  0.7 0.7 copy-done
  1.3 0.7 copy.9.vs
  2.0 0.8 copy.8.wout
  2.8 124.7 %shard_map.64 = f32[1,3072]{1,0:T(1,128)} custom-call(bf16[16,3072]{1,0:T(8,128)(2,1)} %feat.1, bf16[16,256]{1,0:T(8,128)(2,1)} %win.1, bf16[1024,256]{1,0:T(8,128)(2,1)} %wmid.1, f32[256,1]{1,0:T(8,128)} %copy.8.wout, f32[1,3072]{1,0:T(1,128)} %bitcast.5, s32[32,1]{1,0:T(8,128)} %copy.9.vs), custom_call_target="tpu_custom_call" | custom-call | tf_op jit(solution)/shard_map/pallas_call | solution.py:252
  127.5 1.3 %copy.11 = f32[3072]{0:T(1024)} copy(f32[3072]{0:T(1024)} %bitcast.4) | data formatting | bytes 24576
  (1 shorter events, 0.0 us)
Async XLA Ops:
  0.0 0.7 copy-start.1
  0.7 0.7 copy-start

commit v2 on v1

--- a/solution.py
+++ b/solution.py
@@ -11,7 +11,6 @@
 damping = 0.002
 MESH = pl.DeviceIdType.MESH
 NT = (((1,), (1,)), ((), ()))
-TN = (((0,), (0,)), ((), ()))
 
 
 def tile_of(rows):
@@ -20,9 +19,10 @@
 
 def kernel(
     nd, nm, feat, win, wmid, wout, targ, vs, out,
-    win_all, h1t, st, ust, u_row, wmid_t, v_t, rows_out, rows_in, scal_out, scal_in,
-    p_out, p_in, v_all, own, r_p, d_p, q_p,
-    win_ss, win_rs, row_ss, row_rs, scal_ss, scal_rs, p_ss, p_rs, v_ss, v_rs,
+    win_all, win_t, h1t, st, ust, u_row, wmid_t, v_t, rows_out, rows_in, scal_out, scal_in,
+    y_out, y_in, z_out, z_in, v_all, r_p, d_p, q_p,
+    win_ss, win_rs, row_ss, row_rs, scal_ss, scal_rs,
+    y_ss, y_rs, z_ss, z_rs, vy_ss, vy_rs, vz_ss, vz_rs,
 ):
     hidden, cols = wmid.shape
     rows = feat.shape[1]
@@ -31,6 +31,11 @@
     tiles = rows // tile
     dp = lax.axis_index("dp")
     mp = lax.axis_index("mp")
+    nz = nd // 2
+    z, y = dp // 2, lax.rem(dp, 2)
+
+    def rows_of(z_at, y_at):
+        return pl.ds(pl.multiple_of((y_at * nz + z_at) * piece, piece), piece)
 
     barrier = pltpu.get_barrier_semaphore()
 
@@ -68,19 +73,34 @@
             device_id=(lax.rem(dp + d, nd), mp), device_id_type=MESH,
         )
 
-    def p_copy(rnd, d):
-        return pltpu.make_async_remote_copy(
-            src_ref=p_out.at[rnd, d], dst_ref=p_in.at[rnd, d],
-            send_sem=p_ss.at[rnd, d], recv_sem=p_rs.at[rnd, d],
-            device_id=(lax.rem(dp + d, nd), mp), device_id_type=MESH,
-        )
-
-    def v_copy(rnd, d):
-        mine = v_all.at[rnd, pl.ds(pl.multiple_of(dp * piece, piece), piece)]
+    def y_copy(rnd, d):
+        return pltpu.make_async_remote_copy(
+            src_ref=y_out.at[rnd, d], dst_ref=y_in.at[rnd, d],
+            send_sem=y_ss.at[rnd, d], recv_sem=y_rs.at[rnd, d],
+            device_id=(z * 2 + 1 - y, mp), device_id_type=MESH,
+        )
+
+    def z_copy(rnd, d):
+        return pltpu.make_async_remote_copy(
+            src_ref=z_out.at[rnd, d], dst_ref=z_in.at[rnd, d],
+            send_sem=z_ss.at[rnd, d], recv_sem=z_rs.at[rnd, d],
+            device_id=(lax.rem(z + d, nz) * 2 + y, mp), device_id_type=MESH,
+        )
+
+    def vz_copy(rnd, d):
+        mine = v_all.at[rnd, rows_of(z, y)]
         return pltpu.make_async_remote_copy(
             src_ref=mine, dst_ref=mine,
-            send_sem=v_ss.at[rnd, d], recv_sem=v_rs.at[rnd, d],
-            device_id=(lax.rem(dp + d, nd), mp), device_id_type=MESH,
+            send_sem=vz_ss.at[rnd, d], recv_sem=vz_rs.at[rnd, d],
+            device_id=(lax.rem(z + d, nz) * 2 + y, mp), device_id_type=MESH,
+        )
+
+    def vy_copy(rnd, d):
+        theirs = v_all.at[rnd, rows_of(lax.rem(z + nz - d, nz), y)]
+        return pltpu.make_async_remote_copy(
+            src_ref=theirs, dst_ref=theirs,
+            send_sem=vy_ss.at[rnd, d], recv_sem=vy_rs.at[rnd, d],
+            device_id=(z * 2 + 1 - y, mp), device_id_type=MESH,
         )
 
     def start(copy, n):
@@ -129,24 +149,35 @@
     wmid_t[...] = wmid[...].T
     win_all[0] = win[...]
     finish(win_copy, nm)
+    for d in range(nm):
+        owner = lax.rem(mp + nm - d, nm)
+        win_t[pl.ds(pl.multiple_of(owner * cols, cols), cols), :] = win_all[d].T
 
     @pl.loop(0, tiles)
     def _(i):
         at = pl.ds(pl.multiple_of(i * tile, tile), tile)
         block = feat[:, at]
-        for d in range(nm):
-            owner = lax.rem(mp + nm - d, nm)
-            first = lax.dot_general(win_all[d], block, TN, preferred_element_type=jnp.float32)
-            h1t[pl.ds(pl.multiple_of(owner * cols, cols), cols), at] = jnp.tanh(first).astype(
-                jnp.bfloat16
-            )
+        first = jnp.dot(win_t[...], block, preferred_element_type=jnp.float32)
+        h1t[:, at] = jnp.tanh(first).astype(jnp.bfloat16)
         two = jnp.tanh(jnp.dot(wmid_t[...], h1t[:, at], preferred_element_type=jnp.float32))
         weight = wout[...]
         st[:, at] = (1.0 - two * two) * weight
         rows_out[0, :, at] = jnp.sum(two * weight, axis=0, keepdims=True)
 
     def tangent(rnd):
-        finish(functools.partial(v_copy, rnd), nd)
+        @pl.loop(1, nz)
+        def _(d):
+            vz_copy(rnd, d).wait_recv()
+            vy_copy(rnd, d).start()
+
+        @pl.loop(0, nz)
+        def _(d):
+            vy_copy(rnd, d).wait()
+
+        @pl.loop(1, nz)
+        def _(d):
+            vz_copy(rnd, d).wait_send()
+
         v_t[...] = v_all[rnd].T
 
         @pl.loop(0, tiles)
@@ -165,26 +196,40 @@
             at = pl.ds(pl.multiple_of(i * tile, tile), tile)
             ust[:, at] = (u_row[:, at] * st[:, at]).astype(jnp.bfloat16)
 
-        def part(d):
-            owner = lax.rem(dp + d, nd)
-            left = h1t[pl.ds(pl.multiple_of(owner * piece, piece), piece), :]
+        def part(z_at, y_at):
+            left = h1t[rows_of(z_at, y_at), :]
             return lax.dot_general(left, ust[...], NT, preferred_element_type=jnp.float32)
 
-        @pl.loop(1, nd)
-        def _(d):
-            p_out[rnd, d] = part(d).astype(jnp.bfloat16)
-            p_copy(rnd, d).start()
-
-        own[...] = part(0)
-        finish(functools.partial(p_copy, rnd), nd)
-        total = own[...]
-        for d in range(1, nd):
-            total = total + p_in[rnd, d].astype(jnp.float32)
+        @pl.loop(1, nz + 1)
+        def _(i):
+            d = lax.rem(i, nz)
+            y_out[rnd, d] = part(lax.rem(z + d, nz), 1 - y).astype(jnp.bfloat16)
+            y_copy(rnd, d).start()
+
+        @pl.loop(1, nz)
+        def _(d):
+            mine = part(lax.rem(z + d, nz), y)
+            y_copy(rnd, d).wait_recv()
+            z_out[rnd, d] = (mine + y_in[rnd, d].astype(jnp.float32)).astype(jnp.bfloat16)
+            z_copy(rnd, d).start()
+
+        total = part(z, y)
+        y_copy(rnd, 0).wait_recv()
+        total = total + y_in[rnd, 0].astype(jnp.float32)
+        finish(functools.partial(z_copy, rnd), nz)
+        for d in range(1, nz):
+            total = total + z_in[rnd, d].astype(jnp.float32)
+
+        @pl.loop(0, nz)
+        def _(d):
+            y_copy(rnd, d).wait_send()
+
         return total
 
     def spread(rnd):
-        v_all[rnd, pl.ds(pl.multiple_of(dp * piece, piece), piece)] = r_p[...].astype(jnp.bfloat16)
-        start(functools.partial(v_copy, rnd), nd)
+        v_all[rnd, rows_of(z, y)] = r_p[...].astype(jnp.bfloat16)
+        start(functools.partial(vz_copy, rnd), nz)
+        vy_copy(rnd, 0).start()
 
     def dot(a, b):
         return jnp.sum(a * b, axis=1, keepdims=True)
@@ -256,6 +301,7 @@
         out_specs=vmem,
         scratch_shapes=[
             pltpu.VMEM((nm,) + w_in.shape, bf16),
+            pltpu.VMEM((hidden, w_in.shape[0]), bf16),
             pltpu.VMEM((hidden, rows), bf16),
             pltpu.VMEM((cols, rows), f32),
             pltpu.VMEM((cols, rows), bf16),
@@ -266,18 +312,21 @@
             pltpu.VMEM((4, nm, 1, rows), f32),
             pltpu.VMEM((4, 8, 128), f32),
             pltpu.VMEM((4, nd, 8, 128), f32),
-            pltpu.VMEM((3, nd, piece, cols), bf16),
-            pltpu.VMEM((3, nd, piece, cols), bf16),
+            pltpu.VMEM((3, nd // 2, piece, cols), bf16),
+            pltpu.VMEM((3, nd // 2, piece, cols), bf16),
+            pltpu.VMEM((3, nd // 2, piece, cols), bf16),
+            pltpu.VMEM((3, nd // 2, piece, cols), bf16),
             pltpu.VMEM((3, hidden, cols), bf16),
-            pltpu.VMEM((piece, cols), f32),
             pltpu.VMEM((piece, cols), f32),
             pltpu.VMEM((piece, cols), f32),
             pltpu.VMEM((piece, cols), f32),
             dma((nm,)), dma((nm,)),
             dma((4, nm)), dma((4, nm)),
             dma((4, nd)), dma((4, nd)),
-            dma((3, nd)), dma((3, nd)),
-            dma((3, nd)), dma((3, nd)),
+            dma((3, nd // 2)), dma((3, nd // 2)),
+            dma((3, nd // 2)), dma((3, nd // 2)),
+            dma((3, nd // 2)), dma((3, nd // 2)),
+            dma((3, nd // 2)), dma((3, nd // 2)),
         ],
         compiler_params=pltpu.CompilerParams(
             collective_id=0, has_side_effects=True, vmem_limit_bytes=56 * 1024 * 1024

time: 129 us -> 119 us (0.922)
  Pallas kernels: 125 us -> 114 us
    pallas_call x1, Pallas kernels: 125 us -> 114 us  [shards(): pl.pallas_call(functools.partial(kernel, nd, nm), out_shape=jax.ShapeDtyp...]
where the time goes in v2:
time: 119 us; the launch traced here: 118 us
  Pallas kernels  114 us (96%)
  local copies, waits for them, and re-layouts  4.08 us (3%)
    pallas_call x1, Pallas kernels, shards(): pl.pallas_call(functools.partial(kernel, nd, nm), out_shape=jax.ShapeDtyp...  114 us
    unnamed x5, local copies, waits for them, and re-layouts  2.62 us

profile of v2, /device:TPU:0, one launch (start us, length us, event | category | flops | bytes accessed | tf_op | source)
XLA Modules:
  0.0 118.3 jit_solution(9256716537486800805)
XLA Ops:
  0.0 0.0 copy-start.1
  0.0 0.7 copy-done.1
  0.7 0.0 copy-start
  0.7 0.7 copy-done
  1.3 0.7 copy.9.vs
  2.0 0.8 copy.8.wout
  2.8 114.2 %shard_map.64 = f32[1,3072]{1,0:T(1,128)} custom-call(bf16[16,3072]{1,0:T(8,128)(2,1)} %feat.1, bf16[16,256]{1,0:T(8,128)(2,1)} %win.1, bf16[1024,256]{1,0:T(8,128)(2,1)} %wmid.1, f32[256,1]{1,0:T(8,128)} %copy.8.wout, f32[1,3072]{1,0:T(1,128)} %bitcast.5, s32[32,1]{1,0:T(8,128)} %copy.9.vs), custom_call_target="tpu_custom_call" | custom-call | tf_op jit(solution)/shard_map/pallas_call | solution.py:297
  117.0 1.3 %copy.11 = f32[3072]{0:T(1024)} copy(f32[3072]{0:T(1024)} %bitcast.4) | data formatting | bytes 24576
  (1 shorter events, 0.0 us)
Async XLA Ops:
  0.0 0.7 copy-start.1
  0.7 0.7 copy-start

commit v3 on v2

--- a/solution.py
+++ b/solution.py
@@ -17,12 +17,20 @@
     return 512 if rows % 512 == 0 else 128
 
 
+def upright(row):
+    n = row.shape[1]
+    here = lax.broadcasted_iota(jnp.int32, (n, n), 0) == lax.broadcasted_iota(
+        jnp.int32, (n, n), 1
+    )
+    return jnp.sum(jnp.where(here, row, 0.0), axis=1, keepdims=True)
+
+
 def kernel(
     nd, nm, feat, win, wmid, wout, targ, vs, out,
     win_all, win_t, h1t, st, ust, u_row, wmid_t, v_t, rows_out, rows_in, scal_out, scal_in,
     y_out, y_in, z_out, z_in, v_all, r_p, d_p, q_p,
     win_ss, win_rs, row_ss, row_rs, scal_ss, scal_rs,
-    y_ss, y_rs, z_ss, z_rs, vy_ss, vy_rs, vz_ss, vz_rs,
+    y_ss, y_rs, z_ss, z_rs, vy_ss, vy_rs, hop_ss, hop_rs,
 ):
     hidden, cols = wmid.shape
     rows = feat.shape[1]
@@ -87,21 +95,33 @@
             device_id=(lax.rem(z + d, nz) * 2 + y, mp), device_id_type=MESH,
         )
 
-    def vz_copy(rnd, d):
-        mine = v_all.at[rnd, rows_of(z, y)]
-        return pltpu.make_async_remote_copy(
-            src_ref=mine, dst_ref=mine,
-            send_sem=vz_ss.at[rnd, d], recv_sem=vz_rs.at[rnd, d],
-            device_id=(lax.rem(z + d, nz) * 2 + y, mp), device_id_type=MESH,
-        )
-
-    def vy_copy(rnd, d):
-        theirs = v_all.at[rnd, rows_of(lax.rem(z + nz - d, nz), y)]
-        return pltpu.make_async_remote_copy(
-            src_ref=theirs, dst_ref=theirs,
-            send_sem=vy_ss.at[rnd, d], recv_sem=vy_rs.at[rnd, d],
+    def hop_copy(rnd, way, owner):
+        block = v_all.at[rnd, rows_of(owner, y)]
+        z_to = lax.rem(z + 1, nz) if way == 0 else lax.rem(z + nz - 1, nz)
+        return pltpu.make_async_remote_copy(
+            src_ref=block, dst_ref=block,
+            send_sem=hop_ss.at[rnd, way, owner], recv_sem=hop_rs.at[rnd, way, owner],
+            device_id=(z_to * 2 + y, mp), device_id_type=MESH,
+        )
+
+    def vy_copy(rnd, owner):
+        block = v_all.at[rnd, rows_of(owner, y)]
+        return pltpu.make_async_remote_copy(
+            src_ref=block, dst_ref=block,
+            send_sem=vy_ss.at[rnd, owner], recv_sem=vy_rs.at[rnd, owner],
             device_id=(z * 2 + 1 - y, mp), device_id_type=MESH,
         )
+
+    def pass_on(rnd, owner):
+        @pl.when((owner <= z) & (z + 1 < nz))
+        def _():
+            hop_copy(rnd, 0, owner).start()
+
+        @pl.when((owner >= z) & (z > 0))
+        def _():
+            hop_copy(rnd, 1, owner).start()
+
+        vy_copy(rnd, owner).start()
 
     def start(copy, n):
         @pl.loop(1, n)
@@ -137,14 +157,15 @@
         return total
 
     start(win_copy, nm)
-    steps = vs[...]
-    send_scalars(0, [jnp.sum(steps.astype(jnp.float32), axis=0, keepdims=True)])
-    builds = vs.shape[0]
+    steps = upright(vs[...].astype(jnp.float32))
+    out_weight = upright(wout[...].astype(jnp.float32))
+    send_scalars(0, [jnp.sum(steps, axis=0, keepdims=True)])
+    builds = vs.shape[1]
     offset = lax.broadcasted_iota(jnp.int32, (builds, rows), 1) - STEPS * (
         lax.broadcasted_iota(jnp.int32, (builds, rows), 0)
     )
     mask = jnp.sum(
-        jnp.where((offset >= 0) & (offset < steps), 1.0, 0.0), axis=0, keepdims=True
+        jnp.where((offset >= 0) & (offset.astype(jnp.float32) < steps), 1.0, 0.0), axis=0, keepdims=True
     )
     wmid_t[...] = wmid[...].T
     win_all[0] = win[...]
@@ -160,25 +181,41 @@
         first = jnp.dot(win_t[...], block, preferred_element_type=jnp.float32)
         h1t[:, at] = jnp.tanh(first).astype(jnp.bfloat16)
         two = jnp.tanh(jnp.dot(wmid_t[...], h1t[:, at], preferred_element_type=jnp.float32))
-        weight = wout[...]
+        weight = out_weight
         st[:, at] = (1.0 - two * two) * weight
         rows_out[0, :, at] = jnp.sum(two * weight, axis=0, keepdims=True)
 
     def tangent(rnd):
         @pl.loop(1, nz)
         def _(d):
-            vz_copy(rnd, d).wait_recv()
-            vy_copy(rnd, d).start()
+            @pl.when(z - d >= 0)
+            def _():
+                hop_copy(rnd, 0, z - d).wait_recv()
+                pass_on(rnd, z - d)
+
+            @pl.when(z + d < nz)
+            def _():
+                hop_copy(rnd, 1, z + d).wait_recv()
+                pass_on(rnd, z + d)
+
+        half = hidden // 2
+        near = pl.ds(pl.multiple_of(y * half, half), half)
+        far = pl.ds(pl.multiple_of((1 - y) * half, half), half)
+        v_t[:, near] = v_all[rnd, near].T
 
         @pl.loop(0, nz)
-        def _(d):
-            vy_copy(rnd, d).wait()
-
-        @pl.loop(1, nz)
-        def _(d):
-            vz_copy(rnd, d).wait_send()
-
-        v_t[...] = v_all[rnd].T
+        def _(owner):
+            vy_copy(rnd, owner).wait()
+
+            @pl.when((owner <= z) & (z + 1 < nz))
+            def _():
+                hop_copy(rnd, 0, owner).wait_send()
+
+            @pl.when((owner >= z) & (z > 0))
+            def _():
+                hop_copy(rnd, 1, owner).wait_send()
+
+        v_t[:, far] = v_all[rnd, far].T
 
         @pl.loop(0, tiles)
         def _(i):
@@ -228,8 +265,7 @@
 
     def spread(rnd):
         v_all[rnd, rows_of(z, y)] = r_p[...].astype(jnp.bfloat16)
-        start(functools.partial(vz_copy, rnd), nz)
-        vy_copy(rnd, 0).start()
+        pass_on(rnd, z)
 
     def dot(a, b):
         return jnp.sum(a * b, axis=1, keepdims=True)
@@ -326,7 +362,7 @@
             dma((3, nd // 2)), dma((3, nd // 2)),
             dma((3, nd // 2)), dma((3, nd // 2)),
             dma((3, nd // 2)), dma((3, nd // 2)),
-            dma((3, nd // 2)), dma((3, nd // 2)),
+            dma((3, 2, nd // 2)), dma((3, 2, nd // 2)),
         ],
         compiler_params=pltpu.CompilerParams(
             collective_id=0, has_side_effects=True, vmem_limit_bytes=56 * 1024 * 1024
@@ -335,9 +371,9 @@
         features_in,
         w_in,
         w_mid,
-        w_out.astype(f32).reshape(cols, 1),
+        w_out.reshape(1, cols),
         targets.reshape(1, rows),
-        valid_steps.reshape(-1, 1),
+        valid_steps.reshape(1, -1),
     )
     return change.reshape(rows)
 

time: 119 us -> 120 us (level)
  Pallas kernels: 114 us -> 117 us
  local copies, waits for them, and re-layouts: 4.08 us -> 2.53 us
    pallas_call x1, Pallas kernels: 114 us -> 117 us  [shards(): pl.pallas_call(functools.partial(kernel, nd, nm), out_shape=jax.ShapeDtyp...]
    unnamed x5 -> x3, local copies, waits for them, and re-layouts: 2.62 us -> 1.96 us
where the time goes in v3:
time: 120 us
  Pallas kernels  117 us (98%)
  local copies, waits for them, and re-layouts  2.53 us (2%)
    pallas_call x1, Pallas kernels, shards(): pl.pallas_call(functools.partial(kernel, nd, nm), out_shape=jax.ShapeDtyp...  117 us

profile of v3, /device:TPU:0, one launch (start us, length us, event | category | flops | bytes accessed | tf_op | source)
XLA Modules:
  0.0 119.6 jit_solution(8704632350757495641)
XLA Ops:
  0.0 0.0 copy-start
  0.0 0.7 copy-done
  0.7 0.6 reshape.12.wout
  1.2 117.1 %shard_map.64 = f32[1,3072]{1,0:T(1,128)} custom-call(bf16[16,3072]{1,0:T(8,128)(2,1)} %feat.1, bf16[16,256]{1,0:T(8,128)(2,1)} %win.1, bf16[1024,256]{1,0:T(8,128)(2,1)} %wmid.1, bf16[1,256]{1,0:T(2,128)(2,1)} %reshape.12.wout, f32[1,3072]{1,0:T(1,128)} %bitcast.4, s32[1,32]{1,0:T(1,128)} %bitcast.5), custom_call_target="tpu_custom_call" | custom-call | tf_op jit(solution)/shard_map/pallas_call | solution.py:333
  118.3 1.3 %copy.8 = f32[3072]{0:T(1024)} copy(f32[3072]{0:T(1024)} %bitcast.3) | data formatting | bytes 24576
Async XLA Ops:
  0.0 0.7 copy-start
